TPU v7x, 128 devices: a whole 4x4x4 slice. The times are simulated.
128 devices in a mesh: dom: 128 (over x, y, z, core).
Axes of the slice: x: 4, y: 4, z: 4, core: 2. Of those that a mesh axis runs over, the one named last changes fastest.
Arguments:
- density: float32 [1048576], P('dom'), may hold values from 0 to 1
- gradient: float32 [3, 1048576], P(None, 'dom'), may hold values from -3 to 3
- elem_size: float32 [1048576], P('dom'), may hold values from 0.5 to 2
- history: float32 [2, 1048576], P(None, 'dom'), may hold values from -6 to 6
- refine_flags: int32 [1048576], P('dom'), may hold values 0 or 1
- face_neighbor: int32 [6, 1048576], P(None, 'dom'), may hold values from 0 to 12287
- face_weight: float32 [6, 1048576], P(None, 'dom'), may hold values from 0.05 to 0.5
- ghost_send: int32 [512, 1024], P('dom'), may hold values from 0 to 8191
- new_counts: int32 [128], replicated, may hold values from 7168 to 9216, as said below
Outputs:
- indicator: float32 [1048576], P('dom')
- child_fields: float32 [3, 8, 1179648], P(None, None, 'dom')
Inputs may be any that keep to these rules, and one draw needn't show every extreme that they name: `new_counts`: the new partition boundaries b_q lie within 512 elements of q * 8192, so every element moves at most one partition along the curve; some boundary moves by exactly 512 in each direction, and some partition gets 9216 elements.
All inputs are finite; a program needn't handle non-finite values. No bound on the sum of `refine_flags` on one device may be relied on, other than what follows from the above.
Results may differ from a plain program's by a relative error of at most 0.00002.
Values sent between devices are 32-bit elements; how exact they have to be, the bound alone decides.
A program may use at most 128 MiB of HBM per device.

v0:
```python
import jax
import jax.numpy as jnp
from jax import lax
from jax.sharding import PartitionSpec as P


def shifted_2(value, axis, steps):
    count = lax.axis_size(axis)
    pairs = [(source, (source + steps) % count) for source in range(count)]
    return lax.ppermute(value, axis, pairs)


def shifted_3(shard, axis, by):
    length = lax.axis_size(axis)
    pairs = [(i, i + by) for i in range(length) if 0 <= i + by < length]
    return lax.ppermute(shard, axis, pairs)


def prolong(density, gradient, elem_size, history, flags):
    child_ids = jnp.arange(8, dtype=jnp.int32)
    sign_x = (2 * (child_ids % 2) - 1).astype(jnp.float32)[:, None]
    sign_y = (2 * (child_ids // 2 % 2) - 1).astype(jnp.float32)[:, None]
    sign_z = (2 * (child_ids // 4 % 2) - 1).astype(jnp.float32)[:, None]
    slope = (
        sign_x * gradient[0][None, :]
        + sign_y * gradient[1][None, :]
        + sign_z * gradient[2][None, :]
    )
    shifted = density[None, :] + 0.25 * elem_size[None, :] * slope
    refined = (flags > 0)[None, :]
    first_child = (child_ids == 0)[:, None]
    kept_mask = jnp.logical_or(refined, first_child)
    zero_val = jnp.zeros((), jnp.float32)
    density_kids = jnp.where(refined, shifted, jnp.where(first_child, density[None, :], zero_val))
    older = jnp.where(kept_mask, history[0][None, :], zero_val)
    oldest = jnp.where(kept_mask, history[1][None, :], zero_val)
    return jnp.stack([density_kids, older, oldest])


def face_jumps(extended, neighbors, weights, elements):
    across = jnp.take(extended, neighbors.reshape(-1), axis=1).reshape(3, 6, elements)
    own = extended[:, :elements]
    jump = own[:, None, :] - across
    squares = jump[0] * jump[0] + jump[1] * jump[1] + jump[2] * jump[2]
    return jnp.sum(weights * squares, axis=0)


def local(
    density,
    gradient,
    elem_size,
    history,
    refine_flags,
    face_neighbor,
    face_weight,
    ghost_send,
    new_counts,
):
    members = lax.axis_size("dom")
    myself = lax.axis_index("dom")
    elements = density.shape[0]
    margin = elements // 16
    capacity = elements + 2 * margin
    stride_far = members // 8
    offsets = (1, -1, stride_far, -stride_far)
    ghost_rows = jnp.take(gradient, ghost_send, axis=1)
    owner_ids = jnp.arange(members, dtype=jnp.int32)
    zero_int = jnp.zeros((), jnp.int32)
    range_begin = jnp.sum(jnp.where(owner_ids < myself, new_counts, zero_int))
    own_count = jnp.sum(jnp.where(owner_ids == myself, new_counts, zero_int))
    payload = prolong(density, gradient, elem_size, history, refine_flags).reshape(24, elements)
    payload_rows = payload.shape[0]
    front_part = payload[:, :margin]
    back_part = payload[:, elements - margin :]
    ghost_parts = []
    for k in range(4):
        ghost_parts.append(shifted_2(ghost_rows[:, k], "dom", offsets[k]))
    received = jnp.concatenate(ghost_parts, axis=1)
    portions = []
    for stride, portion in ((-1, front_part), (1, back_part)):
        portions.append(shifted_3(portion, "dom", stride))
    extended = jnp.concatenate([gradient, received], axis=1)
    indicator = face_jumps(extended, face_neighbor, face_weight, elements)
    padding = jnp.zeros((payload_rows, 2 * margin), jnp.float32)
    window = jnp.concatenate([portions[1], payload, portions[0], padding], axis=1)
    start = range_begin - myself * elements + margin
    taken = lax.dynamic_slice_in_dim(window, start, capacity, 1)
    slot_ids = jnp.arange(capacity, dtype=jnp.int32)
    zero_val = jnp.zeros((), jnp.float32)
    placed = jnp.where((slot_ids < own_count)[None, :], taken, zero_val)
    return (indicator, placed.reshape(3, 8, capacity))


def solution(mesh):
    placed = (
        P("dom"),
        P(None, "dom"),
        P("dom"),
        P(None, "dom"),
        P("dom"),
        P(None, "dom"),
        P(None, "dom"),
        P("dom", None),
        P(),
    )
    return jax.shard_map(
        local,
        mesh=mesh,
        in_specs=placed,
        out_specs=(P("dom"), P(None, None, "dom")),
        check_vma=False,
    )
```

profile of v0, /device:TPU:6, one launch (start us, length us, event | category | flops | bytes accessed | tf_op | source)
XLA Modules:
  0.0 231.2 jit_solution(10444742640227115172)
XLA Ops:
  0.6 0.0 copy-start
  0.6 0.0 copy-start.6
  0.7 0.0 copy-start.5
  0.7 0.0 copy-start.3
  0.7 0.0 copy-start.4
  0.7 0.0 copy-start.1
  0.7 0.0 copy-start.7
  0.7 0.8 fusion.10
  1.5 0.7 compare_and_fusion.1
  2.2 3.5 %copy.14 = f32[3,8192]{0,1:T(8,128)} copy(f32[3,8192]{1,0:T(4,128)} %param.10) | data formatting | bytes 196608 | tf_op args[1]
  5.7 12.9 %gather_fusion = f32[4096,3]{1,0:T(8,128)S(1)} fusion(f32[3,8192]{0,1:T(8,128)} %copy.14, s32[4096]{0:T(1024)S(1)} %bitcast_clamp_fusion), kind=kCustom, calls=%fused_computation | custom fusion | bytes 114688 | tf_op jit(solution)/shard_map/jit(_take)/gather | solution.py:66
  18.7 0.6 copy.15
  19.3 0.1 collective-permute-start
  19.4 6.3 %collective-permute-start.1 = (f32[3,1024]{1,0:T(4,128)S(1)}, f32[3,1024]{1,0:T(4,128)S(1)}, u32[]{:S(2)}, u32[]{:S(2)}) collective-permute-start(f32[3,1024]{1,0:T(4,128)S(1)} %get-tuple-element.13), channel_id=1, source_target_pairs={{0,127},{1,0},{2,1},{3,2},{4,3},{5,4},{6,5},{7,6},{8,7},{9,8},{10,... | collective-permute-start | bytes 36872 | tf_op jit(solution)/shard_map/ppermute | solution.py:10
  25.7 0.8 collective-permute-start.2
  26.5 3.7 %collective-permute-start.3 = (f32[3,1024]{1,0:T(4,128)S(1)}, f32[3,1024]{1,0:T(4,128)S(1)}, u32[]{:S(2)}, u32[]{:S(2)}) collective-permute-start(f32[3,1024]{1,0:T(4,128)S(1)} %get-tuple-element.11), channel_id=1, source_target_pairs={{0,112},{1,113},{2,114},{3,115},{4,116},{5,117},{6,118},{7,119},{8... | collective-permute-start | bytes 36872 | tf_op jit(solution)/shard_map/ppermute | solution.py:10
  30.1 0.0 copy-done
  30.1 0.1 fusion.25
  30.2 0.0 copy-done.6
  30.3 0.0 copy-done.5
  30.3 0.0 copy-done.3
  30.3 0.1 fusion.26
  30.4 0.0 copy-done.4
  30.4 0.2 select_select_fusion
  30.6 0.1 maximum_bitcast_fusion
  30.7 1.9 collective-permute-start.4
  32.6 0.0 copy-done.1
  32.6 0.1 compare_and_fusion
  32.7 0.2 copy.19
  32.9 0.2 compare_select_fusion
  33.2 0.0 copy-done.7
  33.2 0.6 fusion.11
  34.5 0.1 pad_dynamic-slice_fusion.3
  34.6 0.7 iota_compare_fusion
  35.2 0.0 collective-permute-done
  35.3 7.9 %collective-permute-start.5 = (f32[24,512]{1,0:T(8,128)S(1)}, f32[24,512]{1,0:T(8,128)S(1)}, u32[]{:S(2)}, u32[]{:S(2)}) collective-permute-start(f32[24,512]{1,0:T(8,128)S(1)} %get-tuple-element.4), channel_id=1, source_target_pairs={{1,0},{2,1},{3,2},{4,3},{5,4},{6,5},{7,6},{8,7},{9,8},{10,9},{11,1... | collective-permute-start | bytes 147464 | tf_op jit(solution)/shard_map/ppermute | solution.py:16
  43.1 0.0 collective-permute-done.1
  43.2 0.0 collective-permute-done.2
  43.2 0.0 collective-permute-done.3
  43.2 4.0 %copy.16 = f32[3,12288]{0,1:T(8,128)} copy(f32[3,12288]{1,0:T(4,128)S(1)} %constant_dynamic-update-slice_fusion) | data formatting | bytes 294912 | tf_op jit(solution)/shard_map/concatenate | solution.py:82
  47.2 165.8 %gather_fusion.1 = f32[49152,3]{1,0:T(8,128)} fusion(f32[3,12288]{0,1:T(8,128)} %copy.16, s32[49152]{0:T(1024)S(1)} %broadcast_clamp_fusion), kind=kCustom, calls=%fused_computation.1 | custom fusion | bytes 1376256 | tf_op jit(solution)/shard_map/jit(_take)/gather | solution.py:41
  213.1 15.8 %copy.17 = f32[3,6,8192]{2,1,0:T(8,128)S(1)} copy(f32[3,6,8192]{0,2,1:T(8,128)} %bitcast.38) | data formatting | bytes 1179648 | tf_op jit(solution)/shard_map/jit(_take)/gather | solution.py:41
  228.8 0.1 select_subtract_fusion
  229.0 0.0 copy-done.2
  229.0 0.7 fusion.8
  229.7 0.0 collective-permute-done.4
  229.7 0.0 collective-permute-done.5
  229.7 1.5 fusion.4
  (17 shorter events, 0.2 us)
Async XLA Ops:
  0.6 29.5 %copy-start = (f32[3,8192]{1,0:T(4,128)S(1)}, f32[3,8192]{1,0:T(4,128)}, u32[]{:S(2)}) copy-start(f32[3,8192]{1,0:T(4,128)} %param.10) | copy-start | bytes 294916
  0.6 29.6 %copy-start.6 = (f32[8192]{0:T(1024)S(1)}, f32[8192]{0:T(1024)}, u32[]{:S(2)}) copy-start(f32[8192]{0:T(1024)} %param.11) | copy-start | bytes 98308
  0.7 29.6 %copy-start.5 = (s32[8192]{0:T(1024)S(1)}, s32[8192]{0:T(1024)}, u32[]{:S(2)}) copy-start(s32[8192]{0:T(1024)} %param.13) | copy-start | bytes 98308
  0.7 29.6 %copy-start.3 = (f32[2,8192]{1,0:T(2,128)S(1)}, f32[2,8192]{1,0:T(2,128)}, u32[]{:S(2)}) copy-start(f32[2,8192]{1,0:T(2,128)} %param.12) | copy-start | bytes 196612
  0.7 29.7 %copy-start.4 = (f32[8192]{0:T(1024)S(1)}, f32[8192]{0:T(1024)}, u32[]{:S(2)}) copy-start(f32[8192]{0:T(1024)} %param.9) | copy-start | bytes 98308
  0.7 31.9 %copy-start.1 = (s32[6,8192]{1,0:T(8,128)S(1)}, s32[6,8192]{1,0:T(8,128)}, u32[]{:S(2)}) copy-start(s32[6,8192]{1,0:T(8,128)} %param.14) | copy-start | bytes 589828
  0.7 32.5 %copy-start.7 = (s32[128]{0:T(128)S(1)}, s32[128]{0:T(128)}, u32[]{:S(2)}) copy-start(s32[128]{0:T(128)} %param.17) | copy-start | bytes 1540
  19.3 15.9 %collective-permute-start = (f32[3,1024]{1,0:T(4,128)S(1)}, f32[3,1024]{1,0:T(4,128)S(1)}, u32[]{:S(2)}, u32[]{:S(2)}) collective-permute-start(f32[3,1024]{1,0:T(4,128)S(1)} %get-tuple-element.14), channel_id=1, source_target_pairs={{0,1},{1,2},{2,3},{3,4},{4,5},{5,6},{6,7},{7,8},{8,9},{9,10},{10,1... | collective-permute-start | bytes 36872 | tf_op jit(solution)/shard_map/ppermute | solution.py:10
  19.4 23.7 %collective-permute-start.1 = (f32[3,1024]{1,0:T(4,128)S(1)}, f32[3,1024]{1,0:T(4,128)S(1)}, u32[]{:S(2)}, u32[]{:S(2)}) collective-permute-start(f32[3,1024]{1,0:T(4,128)S(1)} %get-tuple-element.13), channel_id=1, source_target_pairs={{0,127},{1,0},{2,1},{3,2},{4,3},{5,4},{6,5},{7,6},{8,7},{9,8},{10,... | collective-permute-start | bytes 36872 | tf_op jit(solution)/shard_map/ppermute | solution.py:10
  25.7 17.5 %collective-permute-start.2 = (f32[3,1024]{1,0:T(4,128)S(1)}, f32[3,1024]{1,0:T(4,128)S(1)}, u32[]{:S(2)}, u32[]{:S(2)}) collective-permute-start(f32[3,1024]{1,0:T(4,128)S(1)} %get-tuple-element.12), channel_id=1, source_target_pairs={{0,16},{1,17},{2,18},{3,19},{4,20},{5,21},{6,22},{7,23},{8,24},{9,... | collective-permute-start | bytes 36872 | tf_op jit(solution)/shard_map/ppermute | solution.py:10
  26.5 16.7 %collective-permute-start.3 = (f32[3,1024]{1,0:T(4,128)S(1)}, f32[3,1024]{1,0:T(4,128)S(1)}, u32[]{:S(2)}, u32[]{:S(2)}) collective-permute-start(f32[3,1024]{1,0:T(4,128)S(1)} %get-tuple-element.11), channel_id=1, source_target_pairs={{0,112},{1,113},{2,114},{3,115},{4,116},{5,117},{6,118},{7,119},{8... | collective-permute-start | bytes 36872 | tf_op jit(solution)/shard_map/ppermute | solution.py:10
  30.7 199.1 %collective-permute-start.4 = (f32[24,512]{1,0:T(8,128)S(1)}, f32[24,512]{1,0:T(8,128)S(1)}, u32[]{:S(2)}, u32[]{:S(2)}) collective-permute-start(f32[24,512]{1,0:T(8,128)S(1)} %get-tuple-element.5), channel_id=1, source_target_pairs={{0,1},{1,2},{2,3},{3,4},{4,5},{5,6},{6,7},{7,8},{8,9},{9,10},{10,1... | collective-permute-start | bytes 147464 | tf_op jit(solution)/shard_map/ppermute | solution.py:16
  35.3 194.5 %collective-permute-start.5 = (f32[24,512]{1,0:T(8,128)S(1)}, f32[24,512]{1,0:T(8,128)S(1)}, u32[]{:S(2)}, u32[]{:S(2)}) collective-permute-start(f32[24,512]{1,0:T(8,128)S(1)} %get-tuple-element.4), channel_id=1, source_target_pairs={{1,0},{2,1},{3,2},{4,3},{5,4},{6,5},{7,6},{8,7},{9,8},{10,9},{11,1... | collective-permute-start | bytes 147464 | tf_op jit(solution)/shard_map/ppermute | solution.py:16
  213.1 15.9 %copy-start.2 = (f32[6,8192]{1,0:T(8,128)S(1)}, f32[6,8192]{1,0:T(8,128)}, u32[]{:S(2)}) copy-start(f32[6,8192]{1,0:T(8,128)} %param.15) | copy-start | bytes 589828
where the time goes:
time: 232 us; the launch traced here: 231 us
  local copies, waits for them, and re-layouts  203 us (88%)
  starting transfers between devices  20.5 us (9%)
  other arithmetic  5.79 us (2%)
    gather x2, local copies, waits for them, and re-layouts, face_jumps(): jnp.take(extended, neighbors.reshape(-1), axis=1).reshape(3, 6, elements)  182 us
    gather x2, local copies, waits for them, and re-layouts, local(): ghost_rows = jnp.take(gradient, ghost_send, axis=1)  13.6 us
    ppermute x4, starting transfers between devices, shifted_2(): return lax.ppermute(value, axis, pairs)  10.8 us
    ppermute x2, starting transfers between devices, shifted_3(): return lax.ppermute(shard, axis, pairs)  9.78 us
  transfers between devices with their start and end apart: 6, of which 0 were waited for; matrix products, arithmetic and copies ran while one was open for 82% of the time, Pallas kernels for 0%

commit v1 on v0

v1 whole, which is shorter than its diff:
```python
import functools

import jax
import jax.numpy as jnp
from jax import lax
from jax.experimental import pallas as pl
from jax.experimental.pallas import tpu as pltpu
from jax.sharding import PartitionSpec as P

ELEMENTS = 8192
ROWS = ELEMENTS // 128
BLOCKS = ROWS // 8
GHOST = 1024
MARGIN = 512
MARGIN_ROWS = MARGIN // 128
CAPACITY = ELEMENTS + 2 * MARGIN
OUT_ROWS = CAPACITY // 128
FIELDS = 8
OWN_AT = 8
WINDOW = 96
PACKET = 24 + FIELDS * MARGIN_ROWS
FLOAT = jnp.float32


def lookup(row, lanes):
    wide = jnp.broadcast_to(row, (8, 128))
    return jnp.take_along_axis(wide, lanes, axis=1, mode="promise_in_bounds")


def kernel(
    members,
    density,
    gradient,
    elem_size,
    history,
    flags,
    neighbors,
    weights,
    ghost_send,
    counts,
    indicator,
    children,
    density_v,
    gradient_v,
    size_v,
    history_v,
    flags_v,
    neighbors_v,
    weights_v,
    ghost_v,
    counts_v,
    gradient_t,
    history_t,
    neighbors_t,
    weights_t,
    ghost_t,
    found,
    window,
    shifted,
    outgoing,
    incoming,
    local_sems,
    send_sems,
    recv_sems,
):
    me = lax.axis_index("dom")
    far = members // 8
    targets = [lax.rem(me + o + members, members) for o in (1, -1, far, -far)]

    pairs = (
        (gradient, gradient_v),
        (ghost_send, ghost_v),
        (density, density_v),
        (elem_size, size_v),
        (history, history_v),
        (flags, flags_v),
        (neighbors, neighbors_v),
        (counts, counts_v),
        (weights, weights_v),
    )
    copies = [
        pltpu.make_async_copy(source, target, local_sems.at[i])
        for i, (source, target) in enumerate(pairs)
    ]
    for copy in copies:
        copy.start()

    barrier = pltpu.get_barrier_semaphore()
    for target in targets:
        pl.semaphore_signal(
            barrier, inc=1, device_id=(target,), device_id_type=pl.DeviceIdType.MESH
        )

    copies[0].wait()
    copies[1].wait()
    for t in range(8):
        ghost_t[4 * t : 4 * t + 4, :] = ghost_v[:, 128 * t : 128 * t + 128]
    for k in range(4):
        index = ghost_t[pl.ds(k, 8, stride=4), :]
        lanes, rows = index & 127, index >> 7
        totals = [jnp.zeros((8, 128), FLOAT) for _ in range(3)]
        for r in range(ROWS):
            hit = rows == r
            for c in range(3):
                got = lookup(gradient_v[c : c + 1, 128 * r : 128 * r + 128], lanes)
                totals[c] = jnp.where(hit, got, totals[c])
        for c in range(3):
            outgoing[k, 8 * c : 8 * c + 8, :] = totals[c]

    for t in range(ROWS):
        gradient_t[4 * t : 4 * t + 3, :] = gradient_v[:, 128 * t : 128 * t + 128]
    for i in (2, 3, 4, 5):
        copies[i].wait()
    for t in range(ROWS):
        history_t[2 * t : 2 * t + 2, :] = history_v[:, 128 * t : 128 * t + 128]
    for b in range(BLOCKS):
        own = slice(8 * b, 8 * b + 8)
        at = slice(OWN_AT + 8 * b, OWN_AT + 8 * b + 8)
        window[0, at, :] = density_v[own, :]
        for c in range(3):
            window[1 + c, at, :] = gradient_t[pl.ds(32 * b + c, 8, stride=4), :]
        window[4, at, :] = 0.25 * size_v[own, :]
        for c in range(2):
            window[5 + c, at, :] = history_t[pl.ds(16 * b + c, 8, stride=2), :]
        window[7, at, :] = flags_v[own, :].astype(FLOAT)
    for f in range(FIELDS):
        at = 24 + MARGIN_ROWS * f
        last = OWN_AT + ROWS - MARGIN_ROWS
        outgoing[0, at : at + MARGIN_ROWS, :] = window[f, last : last + MARGIN_ROWS, :]
        outgoing[1, at : at + MARGIN_ROWS, :] = window[f, OWN_AT : OWN_AT + MARGIN_ROWS, :]

    pl.semaphore_wait(barrier, 4)
    sends = []
    for k in range(4):
        size = PACKET if k < 2 else 24
        sends.append(
            pltpu.make_async_remote_copy(
                src_ref=outgoing.at[k, pl.ds(0, size)],
                dst_ref=incoming.at[k, pl.ds(0, size)],
                send_sem=send_sems.at[k],
                recv_sem=recv_sems.at[k],
                device_id=(targets[k],),
                device_id_type=pl.DeviceIdType.MESH,
            )
        )
        sends[k].start()

    copies[6].wait()
    for t in range(ROWS):
        neighbors_t[8 * t : 8 * t + 6, :] = neighbors_v[:, 128 * t : 128 * t + 128]

    def own_rows(block, carry):
        base = pl.multiple_of(block * 64, 64)
        for m in range(6):
            index = neighbors_t[pl.ds(base + m, 8, stride=8), :]
            lanes, rows = index & 127, index >> 7
            totals = [jnp.zeros((8, 128), FLOAT) for _ in range(3)]
            for r in range(ROWS):
                hit = rows == r
                for c in range(3):
                    got = lookup(gradient_v[c : c + 1, 128 * r : 128 * r + 128], lanes)
                    totals[c] = jnp.where(hit, got, totals[c])
            for c in range(3):
                found[block, 8 * (3 * m + c) : 8 * (3 * m + c) + 8, :] = totals[c]
        return carry

    lax.fori_loop(0, BLOCKS, own_rows, 0)

    for send in sends:
        send.wait()
    copies[8].wait()
    for t in range(ROWS):
        weights_t[8 * t : 8 * t + 6, :] = weights_v[:, 128 * t : 128 * t + 128]

    def ghost_rows(block, carry):
        base = pl.multiple_of(block * 64, 64)
        own = [gradient_t[pl.ds(pl.multiple_of(block * 32, 32) + c, 8, stride=4), :] for c in range(3)]
        result = jnp.zeros((8, 128), FLOAT)
        for m in range(6):
            index = neighbors_t[pl.ds(base + m, 8, stride=8), :]
            lanes, rows = index & 127, index >> 7
            totals = [found[block, 8 * (3 * m + c) : 8 * (3 * m + c) + 8, :] for c in range(3)]
            for k in range(4):
                for s in range(8):
                    hit = rows == ROWS + 8 * k + s
                    for c in range(3):
                        got = lookup(incoming[k, 8 * c + s : 8 * c + s + 1, :], lanes)
                        totals[c] = jnp.where(hit, got, totals[c])
            square = None
            for c in range(3):
                jump = own[c] - totals[c]
                square = jump * jump if square is None else square + jump * jump
            result = result + weights_t[pl.ds(base + m, 8, stride=8), :] * square
        indicator[pl.ds(pl.multiple_of(block * 8, 8), 8), :] = result
        return carry

    lax.fori_loop(0, BLOCKS, ghost_rows, 0)

    for f in range(FIELDS):
        at = 24 + MARGIN_ROWS * f
        window[f, OWN_AT - MARGIN_ROWS : OWN_AT, :] = incoming[0, at : at + MARGIN_ROWS, :]
        right = OWN_AT + ROWS
        window[f, right : right + 8, :] = jnp.zeros((8, 128), FLOAT)
        window[f, right + 8 : right + 16, :] = jnp.zeros((8, 128), FLOAT)
        window[f, right : right + MARGIN_ROWS, :] = incoming[1, at : at + MARGIN_ROWS, :]
    copies[7].wait()
    owners = lax.broadcasted_iota(jnp.int32, (1, 128), 1)
    held = counts_v[...]
    begin = jnp.sum(jnp.where(owners < me, held, 0))
    count = jnp.sum(jnp.where(owners == me, held, 0))
    count = jnp.minimum(count, members * ELEMENTS - begin)
    start = jnp.clip(begin - me * ELEMENTS + MARGIN, 0, 2 * MARGIN)
    first, turn = start // 128, start % 128
    first = first + OWN_AT - MARGIN_ROWS
    lane = lax.broadcasted_iota(jnp.int32, (8, 128), 1)
    slot = lax.broadcasted_iota(jnp.int32, (8, 128), 0) * 128 + lane
    turned = (lane + turn) & 127
    low = lane < 128 - turn
    for f in range(FIELDS):
        for b in range(OUT_ROWS // 8):
            here = window[f, pl.ds(first + 8 * b, 8), :]
            there = window[f, pl.ds(first + 8 * b + 1, 8), :]
            both = [jnp.take_along_axis(v, turned, axis=1, mode="promise_in_bounds") for v in (here, there)]
            value = jnp.where(low, both[0], both[1])
            if f in (0, 5, 6, 7):
                value = jnp.where(slot + 1024 * b < count, value, 0.0)
            shifted[f, 8 * b : 8 * b + 8, :] = value

    child = lax.broadcasted_iota(jnp.int32, (8, 128), 0)
    signs = [(2 * ((child >> c) & 1) - 1).astype(FLOAT) for c in range(3)]
    eldest = child == 0
    for t in range(OUT_ROWS):
        row = [jnp.broadcast_to(shifted[f, t : t + 1, :], (8, 128)) for f in range(FIELDS)]
        slope = signs[0] * row[1] + signs[1] * row[2] + signs[2] * row[3]
        refined = row[7] > 0.0
        kept = jnp.logical_or(refined, eldest)
        at = slice(128 * t, 128 * t + 128)
        moved = jnp.where(refined, row[0] + row[4] * slope, row[0])
        children[0, :, at] = jnp.where(kept, moved, 0.0)
        children[1, :, at] = jnp.where(kept, row[5], 0.0)
        children[2, :, at] = jnp.where(kept, row[6], 0.0)


def local(
    members,
    density,
    gradient,
    elem_size,
    history,
    refine_flags,
    face_neighbor,
    face_weight,
    ghost_send,
    new_counts,
):
    vmem = pltpu.VMEM
    flat = (ROWS, 128)
    indicator, children = pl.pallas_call(
        functools.partial(kernel, members),
        out_shape=(
            jax.ShapeDtypeStruct(flat, FLOAT),
            jax.ShapeDtypeStruct((3, 8, CAPACITY), FLOAT),
        ),
        in_specs=[pl.BlockSpec(memory_space=pl.ANY)] * 9,
        out_specs=(pl.BlockSpec(memory_space=vmem),) * 2,
        scratch_shapes=[
            vmem(flat, FLOAT),
            vmem((3, ELEMENTS), FLOAT),
            vmem(flat, FLOAT),
            vmem((2, ELEMENTS), FLOAT),
            vmem(flat, jnp.int32),
            vmem((6, ELEMENTS), jnp.int32),
            vmem((6, ELEMENTS), FLOAT),
            vmem((4, GHOST), jnp.int32),
            vmem((1, 128), jnp.int32),
            vmem((4 * ROWS, 128), FLOAT),
            vmem((2 * ROWS, 128), FLOAT),
            vmem((8 * ROWS, 128), jnp.int32),
            vmem((8 * ROWS, 128), FLOAT),
            vmem((32, 128), jnp.int32),
            vmem((BLOCKS, 144, 128), FLOAT),
            vmem((FIELDS, WINDOW, 128), FLOAT),
            vmem((FIELDS, OUT_ROWS, 128), FLOAT),
            vmem((4, PACKET, 128), FLOAT),
            vmem((4, PACKET, 128), FLOAT),
            pltpu.SemaphoreType.DMA((9,)),
            pltpu.SemaphoreType.DMA((4,)),
            pltpu.SemaphoreType.DMA((4,)),
        ],
        compiler_params=pltpu.CompilerParams(
            collective_id=0, has_side_effects=True, vmem_limit_bytes=32 * 1024 * 1024
        ),
    )(
        density.reshape(flat),
        gradient,
        elem_size.reshape(flat),
        history,
        refine_flags.reshape(flat),
        face_neighbor,
        face_weight,
        ghost_send,
        new_counts.reshape(1, 128),
    )
    return indicator.reshape(ELEMENTS), children


def solution(mesh):
    placed = (
        P("dom"),
        P(None, "dom"),
        P("dom"),
        P(None, "dom"),
        P("dom"),
        P(None, "dom"),
        P(None, "dom"),
        P("dom", None),
        P(),
    )
    return jax.shard_map(
        functools.partial(local, mesh.shape["dom"]),
        mesh=mesh,
        in_specs=placed,
        out_specs=(P("dom"), P(None, None, "dom")),
        check_vma=False,
    )
```

time: 232 us -> 35.4 us (0.15)
  the two profiles are of different devices: /device:TPU:6 before, /device:TPU:0 now
where the time goes in v1:
time: 35.4 us; the launch traced here: 34.9 us
  Pallas kernels  25.4 us (72%)
  local copies, waits for them, and re-layouts  8.81 us (25%)
  between operations  0.66 us (2%)
    pallas_call x1, Pallas kernels, local(): pl.pallas_call(functools.partial(kernel, members), out_shape=(jax.ShapeDt...  25.4 us
    unnamed x20, local copies, waits for them, and re-layouts  8.81 us

profile of v1, /device:TPU:0, one launch (start us, length us, event | category | flops | bytes accessed | tf_op | source)
XLA Modules:
  0.0 34.9 jit_solution(7104392556217929663)
XLA Ops:
  0.6 0.0 copy-start.8
  0.6 0.6 %copy-done.8 = s32[128]{0:T(128)S(1)} copy-done((s32[128]{0:T(128)S(1)}, s32[128]{0:T(128)}, u32[]{:S(2)}) %copy-start.8) | copy-done | bytes 536
  1.3 0.0 copy-start
  1.3 0.9 %copy-done = s32[6,8192]{1,0:T(8,128)S(1)} copy-done((s32[6,8192]{1,0:T(8,128)S(1)}, s32[6,8192]{1,0:T(8,128)}, u32[]{:S(2)}) %copy-start) | copy-done | bytes 196632
  2.2 0.0 copy-start.1
  2.2 0.9 %copy-done.1 = f32[6,8192]{1,0:T(8,128)S(1)} copy-done((f32[6,8192]{1,0:T(8,128)S(1)}, f32[6,8192]{1,0:T(8,128)}, u32[]{:S(2)}) %copy-start.1) | copy-done | bytes 196632
  3.2 0.0 copy-start.2
  3.2 0.9 %copy-done.2 = f32[3,8192]{1,0:T(4,128)S(1)} copy-done((f32[3,8192]{1,0:T(4,128)S(1)}, f32[3,8192]{1,0:T(4,128)}, u32[]{:S(2)}) %copy-start.2) | copy-done | bytes 98328
  4.1 0.0 copy-start.3
  4.1 0.8 %copy-done.3 = f32[2,8192]{1,0:T(2,128)S(1)} copy-done((f32[2,8192]{1,0:T(2,128)S(1)}, f32[2,8192]{1,0:T(2,128)}, u32[]{:S(2)}) %copy-start.3) | copy-done | bytes 65560
  4.9 0.0 copy-start.4
  4.9 0.8 %copy-done.4 = f32[8192]{0:T(1024)S(1)} copy-done((f32[8192]{0:T(1024)S(1)}, f32[8192]{0:T(1024)}, u32[]{:S(2)}) %copy-start.4) | copy-done | bytes 32792
  5.7 0.0 copy-start.5
  5.7 0.8 %copy-done.5 = f32[8192]{0:T(1024)S(1)} copy-done((f32[8192]{0:T(1024)S(1)}, f32[8192]{0:T(1024)}, u32[]{:S(2)}) %copy-start.5) | copy-done | bytes 32792
  6.5 0.0 copy-start.6
  6.5 0.8 %copy-done.6 = s32[8192]{0:T(1024)S(1)} copy-done((s32[8192]{0:T(1024)S(1)}, s32[8192]{0:T(1024)}, u32[]{:S(2)}) %copy-start.6) | copy-done | bytes 32792
  7.2 0.0 copy-start.7
  7.2 0.7 %copy-done.7 = s32[4,1024]{1,0:T(4,128)S(1)} copy-done((s32[4,1024]{1,0:T(4,128)S(1)}, s32[4,1024]{1,0:T(4,128)}, u32[]{:S(2)}) %copy-start.7) | copy-done | bytes 16408
  7.9 25.4 %shard_map.104 = (f32[64,128]{1,0:T(8,128)S(1)}, f32[3,8,9216]{2,1,0:T(8,128)S(1)}) custom-call(f32[64,128]{1,0:T(8,128)S(1)} %bitcast.5, f32[3,8192]{1,0:T(4,128)S(1)} %copy-done.2, f32[64,128]{1,0:T(8,128)S(1)} %bitcast.6, f32[2,8192]{1,0:T(2,128)S(1)} %copy-done.3, s32[64,128]{1,0:T(8,128)S(1)} %bitcast.7, s32[6,8192]{1,0:T(8,128)S(1)} %copy-done, ...), custom_call_target="tpu_custom_call" | custom-call | tf_op jit(solution)/shard_map/pallas_call | solution.py:258
  33.3 0.6 %copy.13 = f32[8192]{0:T(1024)} copy(f32[8192]{0:T(1024)S(1)} %bitcast.8) | data formatting | bytes 65536
  33.9 0.9 %copy.14 = f32[3,8,9216]{2,1,0:T(8,128)} copy(f32[3,8,9216]{2,1,0:T(8,128)S(1)} %get-tuple-element.9) | data formatting | bytes 1769472
Async XLA Ops:
  0.6 0.7 %copy-start.8 = (s32[128]{0:T(128)S(1)}, s32[128]{0:T(128)}, u32[]{:S(2)}) copy-start(s32[128]{0:T(128)} %param.17) | copy-start | bytes 1540
  1.3 0.9 %copy-start = (s32[6,8192]{1,0:T(8,128)S(1)}, s32[6,8192]{1,0:T(8,128)}, u32[]{:S(2)}) copy-start(s32[6,8192]{1,0:T(8,128)} %neighbors.1) | copy-start | bytes 589828
  2.2 0.9 %copy-start.1 = (f32[6,8192]{1,0:T(8,128)S(1)}, f32[6,8192]{1,0:T(8,128)}, u32[]{:S(2)}) copy-start(f32[6,8192]{1,0:T(8,128)} %weights.1) | copy-start | bytes 589828
  3.2 0.9 %copy-start.2 = (f32[3,8192]{1,0:T(4,128)S(1)}, f32[3,8192]{1,0:T(4,128)}, u32[]{:S(2)}) copy-start(f32[3,8192]{1,0:T(4,128)} %gradient.1) | copy-start | bytes 294916
  4.1 0.8 %copy-start.3 = (f32[2,8192]{1,0:T(2,128)S(1)}, f32[2,8192]{1,0:T(2,128)}, u32[]{:S(2)}) copy-start(f32[2,8192]{1,0:T(2,128)} %history.1) | copy-start | bytes 196612
  4.9 0.8 %copy-start.4 = (f32[8192]{0:T(1024)S(1)}, f32[8192]{0:T(1024)}, u32[]{:S(2)}) copy-start(f32[8192]{0:T(1024)} %param.9) | copy-start | bytes 98308
  5.7 0.8 %copy-start.5 = (f32[8192]{0:T(1024)S(1)}, f32[8192]{0:T(1024)}, u32[]{:S(2)}) copy-start(f32[8192]{0:T(1024)} %param.11) | copy-start | bytes 98308
  6.5 0.8 %copy-start.6 = (s32[8192]{0:T(1024)S(1)}, s32[8192]{0:T(1024)}, u32[]{:S(2)}) copy-start(s32[8192]{0:T(1024)} %param.13) | copy-start | bytes 98308
  7.2 0.7 %copy-start.7 = (s32[4,1024]{1,0:T(4,128)S(1)}, s32[4,1024]{1,0:T(4,128)}, u32[]{:S(2)}) copy-start(s32[4,1024]{1,0:T(4,128)} %ghost_send.1) | copy-start | bytes 49156

commit v2 on v1

--- a/solution.py
+++ b/solution.py
@@ -255,13 +255,25 @@
 ):
     vmem = pltpu.VMEM
     flat = (ROWS, 128)
+    operands = (
+        density.reshape(flat),
+        gradient,
+        elem_size.reshape(flat),
+        history,
+        refine_flags.reshape(flat),
+        face_neighbor,
+        face_weight,
+        ghost_send,
+        new_counts.reshape(1, 128),
+    )
+    operands = [pltpu.with_memory_space_constraint(x, pltpu.HBM) for x in operands]
     indicator, children = pl.pallas_call(
         functools.partial(kernel, members),
         out_shape=(
             jax.ShapeDtypeStruct(flat, FLOAT),
             jax.ShapeDtypeStruct((3, 8, CAPACITY), FLOAT),
         ),
-        in_specs=[pl.BlockSpec(memory_space=pl.ANY)] * 9,
+        in_specs=[pl.BlockSpec(memory_space=pltpu.HBM)] * 9,
         out_specs=(pl.BlockSpec(memory_space=vmem),) * 2,
         scratch_shapes=[
             vmem(flat, FLOAT),
@@ -290,17 +302,7 @@
         compiler_params=pltpu.CompilerParams(
             collective_id=0, has_side_effects=True, vmem_limit_bytes=32 * 1024 * 1024
         ),
-    )(
-        density.reshape(flat),
-        gradient,
-        elem_size.reshape(flat),
-        history,
-        refine_flags.reshape(flat),
-        face_neighbor,
-        face_weight,
-        ghost_send,
-        new_counts.reshape(1, 128),
-    )
+    )(*operands)
     return indicator.reshape(ELEMENTS), children
 
 

time: 35.4 us -> 27.4 us (0.77); the launches traced: 34.9 us -> 27.2 us
  local copies, waits for them, and re-layouts: 8.81 us -> 1.53 us
    unnamed x20 -> x2, local copies, waits for them, and re-layouts: 8.81 us -> 1.53 us
where the time goes in v2:
time: 27.4 us; the launch traced here: 27.2 us
  Pallas kernels  25.1 us (92%)
  local copies, waits for them, and re-layouts  1.53 us (6%)
  between operations  0.64 us (2%)
    pallas_call x1, Pallas kernels, local(): pl.pallas_call(functools.partial(kernel, members), out_shape=(jax.ShapeDt...  25.1 us
    unnamed x2, local copies, waits for them, and re-layouts  1.53 us

profile of v2, /device:TPU:0, one launch (start us, length us, event | category | flops | bytes accessed | tf_op | source)
XLA Modules:
  0.0 27.2 jit_solution(14904064831469497464)
XLA Ops:
  0.6 25.1 %shard_map.104 = (f32[64,128]{1,0:T(8,128)S(1)}, f32[3,8,9216]{2,1,0:T(8,128)S(1)}) custom-call(f32[64,128]{1,0:T(8,128)} %bitcast.6, f32[3,8192]{1,0:T(4,128)} %gradient.1, f32[64,128]{1,0:T(8,128)} %bitcast.7, f32[2,8192]{1,0:T(2,128)} %history.1, s32[64,128]{1,0:T(8,128)} %bitcast.8, s32[6,8192]{1,0:T(8,128)} %neighbors.1, f32[6,8192]{1,0:T(8,128)} %weights.1, ...), custom_call_target="tpu_custom_call" | custom-call | tf_op jit(solution)/shard_map/pallas_call | solution.py:270
  25.7 0.6 %copy.13 = f32[8192]{0:T(1024)} copy(f32[8192]{0:T(1024)S(1)} %bitcast.5) | data formatting | bytes 65536
  26.3 0.9 %copy.14 = f32[3,8,9216]{2,1,0:T(8,128)} copy(f32[3,8,9216]{2,1,0:T(8,128)S(1)} %get-tuple-element.9) | data formatting | bytes 1769472

commit v3 on v2

--- a/solution.py
+++ b/solution.py
@@ -54,7 +54,12 @@
     neighbors_t,
     weights_t,
     ghost_t,
-    found,
+    column_t,
+    row_t,
+    table,
+    steps,
+    own_sum,
+    terms,
     window,
     shifted,
     outgoing,
@@ -146,55 +151,103 @@
         sends[k].start()
 
     copies[6].wait()
-    for t in range(ROWS):
-        neighbors_t[8 * t : 8 * t + 6, :] = neighbors_v[:, 128 * t : 128 * t + 128]
-
-    def own_rows(block, carry):
-        base = pl.multiple_of(block * 64, 64)
-        for m in range(6):
-            index = neighbors_t[pl.ds(base + m, 8, stride=8), :]
-            lanes, rows = index & 127, index >> 7
-            totals = [jnp.zeros((8, 128), FLOAT) for _ in range(3)]
-            for r in range(ROWS):
-                hit = rows == r
-                for c in range(3):
-                    got = lookup(gradient_v[c : c + 1, 128 * r : 128 * r + 128], lanes)
-                    totals[c] = jnp.where(hit, got, totals[c])
-            for c in range(3):
-                found[block, 8 * (3 * m + c) : 8 * (3 * m + c) + 8, :] = totals[c]
-        return carry
-
-    lax.fori_loop(0, BLOCKS, own_rows, 0)
-
-    for send in sends:
-        send.wait()
     copies[8].wait()
     for t in range(ROWS):
+        index = neighbors_v[:, 128 * t : 128 * t + 128]
+        neighbors_t[8 * t : 8 * t + 6, :] = index
+        half = (index >> 12) & 1
+        column_t[8 * t : 8 * t + 6, :] = ((index & 127) + 128 * half + 256 * (index >> 13)).astype(FLOAT)
+        row_t[8 * t : 8 * t + 6, :] = (index >> 7) & 31
         weights_t[8 * t : 8 * t + 6, :] = weights_v[:, 128 * t : 128 * t + 128]
-
-    def ghost_rows(block, carry):
+    for c in range(3):
+        for half in range(2):
+            for q in range(2):
+                part = jnp.concatenate(
+                    [gradient_t[pl.ds(4 * (32 * half + 16 * q + 8 * u) + c, 8, stride=4), :] for u in range(2)], axis=0
+                )
+                for s in range(3):
+                    piece = part.astype(jnp.bfloat16)
+                    at = 96 * s + 32 * c + 16 * q
+                    table[at : at + 16, 128 * half : 128 * half + 128] = piece
+                    part = part - piece.astype(FLOAT)
+    steps[...] = lax.broadcasted_iota(jnp.int32, (256, 128), 0).astype(FLOAT).astype(jnp.bfloat16)
+    sublane = lax.broadcasted_iota(jnp.int32, (8, 128), 0)
+    one, zero = jnp.ones((), jnp.bfloat16), jnp.zeros((), jnp.bfloat16)
+
+    def wide(ref, at):
+        return jnp.broadcast_to(ref[pl.ds(at, 1), :], (8, 128))
+
+    def own_block(block):
+        for p in range(4):
+            sums = [jnp.zeros((8, 128), FLOAT) for _ in range(2)]
+            rows = [8 * block + 2 * p + e for e in range(2)]
+            for m in range(6):
+                hot = []
+                for e in range(2):
+                    column = jnp.broadcast_to(column_t[pl.ds(8 * rows[e] + m, 1), :], (16, 128))
+                    column = jnp.concatenate([column.astype(jnp.bfloat16)] * 16, axis=0)
+                    hot.append(jnp.where(column == steps[...], one, zero))
+                hot = jnp.concatenate(hot, axis=1)
+                got = jnp.dot(table[...], hot, preferred_element_type=FLOAT)
+                got = got[0:96] + got[96:192] + got[192:288]
+                for e in range(2):
+                    row = wide(row_t, 8 * rows[e] + m)
+                    hits = [row == sublane + 8 * g for g in range(4)]
+                    square = None
+                    for c in range(3):
+                        value = jnp.zeros((8, 128), FLOAT)
+                        for g in range(4):
+                            at = 32 * c + 8 * g
+                            value = jnp.where(hits[g], got[at : at + 8, 128 * e : 128 * e + 128], value)
+                        jump = wide(gradient_t, 4 * rows[e] + c) - value
+                        square = jump * jump if square is None else square + jump * jump
+                    here = jnp.logical_and((row & 7) == sublane, wide(column_t, 8 * rows[e] + m) < 256.0)
+                    sums[e] = sums[e] + jnp.where(here, wide(weights_t, 8 * rows[e] + m) * square, 0.0)
+            for e in range(2):
+                own_sum[pl.ds(rows[e], 1), :] = jnp.sum(sums[e], axis=0, keepdims=True)
+
+    def ghost_unit(unit, odd):
+        block = unit // 6
+        m = unit - 6 * block
         base = pl.multiple_of(block * 64, 64)
-        own = [gradient_t[pl.ds(pl.multiple_of(block * 32, 32) + c, 8, stride=4), :] for c in range(3)]
-        result = jnp.zeros((8, 128), FLOAT)
+        index = neighbors_t[pl.ds(base + m, 8, stride=8), :]
+        lanes, rows = index & 127, index >> 7
+        totals = [jnp.zeros((8, 128), FLOAT) for _ in range(3)]
+        for k in (odd, 2 + odd):
+            for s in range(8):
+                hit = rows == ROWS + 8 * k + s
+                for c in range(3):
+                    got = lookup(incoming[k, 8 * c + s : 8 * c + s + 1, :], lanes)
+                    totals[c] = jnp.where(hit, got, totals[c])
+        square = None
+        for c in range(3):
+            jump = gradient_t[pl.ds(pl.multiple_of(block * 32, 32) + c, 8, stride=4), :] - totals[c]
+            square = jump * jump if square is None else square + jump * jump
+        here = jnp.logical_and(rows >= ROWS, ((rows >> 3) & 1) == odd)
+        terms[odd, unit] = jnp.where(here, weights_t[pl.ds(base + m, 8, stride=8), :] * square, 0.0)
+
+    def alone(block, carry):
+        own_block(block)
+        return carry
+
+    def beside(odd, first_block, step, carry):
+        for v in range(16):
+            ghost_unit(16 * step + v, odd)
+        own_block(first_block + step)
+        return carry
+
+    lax.fori_loop(0, 2, alone, 0)
+    sends[1].wait_recv()
+    sends[3].wait_recv()
+    lax.fori_loop(0, 3, functools.partial(beside, 1, 2), 0)
+    sends[0].wait_recv()
+    sends[2].wait_recv()
+    lax.fori_loop(0, 3, functools.partial(beside, 0, 5), 0)
+    for block in range(BLOCKS):
+        total = own_sum[8 * block : 8 * block + 8, :]
         for m in range(6):
-            index = neighbors_t[pl.ds(base + m, 8, stride=8), :]
-            lanes, rows = index & 127, index >> 7
-            totals = [found[block, 8 * (3 * m + c) : 8 * (3 * m + c) + 8, :] for c in range(3)]
-            for k in range(4):
-                for s in range(8):
-                    hit = rows == ROWS + 8 * k + s
-                    for c in range(3):
-                        got = lookup(incoming[k, 8 * c + s : 8 * c + s + 1, :], lanes)
-                        totals[c] = jnp.where(hit, got, totals[c])
-            square = None
-            for c in range(3):
-                jump = own[c] - totals[c]
-                square = jump * jump if square is None else square + jump * jump
-            result = result + weights_t[pl.ds(base + m, 8, stride=8), :] * square
-        indicator[pl.ds(pl.multiple_of(block * 8, 8), 8), :] = result
-        return carry
-
-    lax.fori_loop(0, BLOCKS, ghost_rows, 0)
+            total = total + (terms[0, 6 * block + m] + terms[1, 6 * block + m])
+        indicator[8 * block : 8 * block + 8, :] = total
 
     for f in range(FIELDS):
         at = 24 + MARGIN_ROWS * f
@@ -239,6 +292,8 @@
         children[0, :, at] = jnp.where(kept, moved, 0.0)
         children[1, :, at] = jnp.where(kept, row[5], 0.0)
         children[2, :, at] = jnp.where(kept, row[6], 0.0)
+    for send in sends:
+        send.wait_send()
 
 
 def local(
@@ -290,7 +345,12 @@
             vmem((8 * ROWS, 128), jnp.int32),
             vmem((8 * ROWS, 128), FLOAT),
             vmem((32, 128), jnp.int32),
-            vmem((BLOCKS, 144, 128), FLOAT),
+            vmem((8 * ROWS, 128), FLOAT),
+            vmem((8 * ROWS, 128), jnp.int32),
+            vmem((288, 256), jnp.bfloat16),
+            vmem((256, 128), jnp.bfloat16),
+            vmem(flat, FLOAT),
+            vmem((2, 6 * BLOCKS, 8, 128), FLOAT),
             vmem((FIELDS, WINDOW, 128), FLOAT),
             vmem((FIELDS, OUT_ROWS, 128), FLOAT),
             vmem((4, PACKET, 128), FLOAT),

time: 27.4 us -> 20.6 us (0.75)
  Pallas kernels: 25.1 us -> 18.3 us
    pallas_call x1, Pallas kernels: 25.1 us -> 18.3 us  [local(): pl.pallas_call(functools.partial(kernel, members), out_shape=(jax.ShapeDt...]
where the time goes in v3:
time: 20.6 us; the launch traced here: 20.5 us
  Pallas kernels  18.3 us (89%)
  local copies, waits for them, and re-layouts  1.53 us (7%)
  between operations  0.64 us (3%)
    pallas_call x1, Pallas kernels, local(): pl.pallas_call(functools.partial(kernel, members), out_shape=(jax.ShapeDt...  18.3 us
    unnamed x2, local copies, waits for them, and re-layouts  1.53 us

profile of v3, /device:TPU:0, one launch (start us, length us, event | category | flops | bytes accessed | tf_op | source)
XLA Modules:
  0.0 20.5 jit_solution(3990733009393086295)
XLA Ops:
  0.6 18.3 %shard_map.104 = (f32[64,128]{1,0:T(8,128)S(1)}, f32[3,8,9216]{2,1,0:T(8,128)S(1)}) custom-call(f32[64,128]{1,0:T(8,128)} %bitcast.6, f32[3,8192]{1,0:T(4,128)} %gradient.1, f32[64,128]{1,0:T(8,128)} %bitcast.7, f32[2,8192]{1,0:T(2,128)} %history.1, s32[64,128]{1,0:T(8,128)} %bitcast.8, s32[6,8192]{1,0:T(8,128)} %neighbors.1, f32[6,8192]{1,0:T(8,128)} %weights.1, ...), custom_call_target="tpu_custom_call" | custom-call | tf_op jit(solution)/shard_map/pallas_call | solution.py:325
  19.0 0.6 %copy.13 = f32[8192]{0:T(1024)} copy(f32[8192]{0:T(1024)S(1)} %bitcast.5) | data formatting | bytes 65536
  19.6 0.9 %copy.14 = f32[3,8,9216]{2,1,0:T(8,128)} copy(f32[3,8,9216]{2,1,0:T(8,128)S(1)} %get-tuple-element.9) | data formatting | bytes 1769472

commit v4 on v3

--- a/solution.py
+++ b/solution.py
@@ -67,6 +67,7 @@
     local_sems,
     send_sems,
     recv_sems,
+    ready_sems,
 ):
     me = lax.axis_index("dom")
     far = members // 8
@@ -87,14 +88,22 @@
         pltpu.make_async_copy(source, target, local_sems.at[i])
         for i, (source, target) in enumerate(pairs)
     ]
-    for copy in copies:
+    for copy in copies[:2]:
         copy.start()
 
+    offsets = (1, -1, far, -far)
+    mesh_id = pl.DeviceIdType.MESH
     barrier = pltpu.get_barrier_semaphore()
-    for target in targets:
-        pl.semaphore_signal(
-            barrier, inc=1, device_id=(target,), device_id_type=pl.DeviceIdType.MESH
+    for k in range(4):
+        announce = functools.partial(
+            pl.semaphore_signal, barrier, inc=1, device_id=(targets[k],), device_id_type=mesh_id
         )
+        if offsets[k] > 0:
+            pl.when(me + offsets[k] < members)(announce)
+        else:
+            announce()
+    for copy in copies[2:]:
+        copy.start()
 
     copies[0].wait()
     copies[1].wait()
@@ -134,7 +143,12 @@
         outgoing[0, at : at + MARGIN_ROWS, :] = window[f, last : last + MARGIN_ROWS, :]
         outgoing[1, at : at + MARGIN_ROWS, :] = window[f, OWN_AT : OWN_AT + MARGIN_ROWS, :]
 
-    pl.semaphore_wait(barrier, 4)
+    pl.semaphore_wait(barrier, 4 - (me < far).astype(jnp.int32) - (me < 1).astype(jnp.int32))
+    for k in (0, 2):
+        answer = functools.partial(
+            pl.semaphore_signal, ready_sems.at[k + 1], inc=1, device_id=(targets[k],), device_id_type=mesh_id
+        )
+        pl.when(me + offsets[k] >= members)(answer)
     sends = []
     for k in range(4):
         size = PACKET if k < 2 else 24
@@ -145,10 +159,21 @@
                 send_sem=send_sems.at[k],
                 recv_sem=recv_sems.at[k],
                 device_id=(targets[k],),
-                device_id_type=pl.DeviceIdType.MESH,
+                device_id_type=mesh_id,
             )
         )
-        sends[k].start()
+        if offsets[k] > 0:
+            sends[k].start()
+        else:
+            pl.when(me + offsets[k] >= 0)(sends[k].start)
+
+    def send_late():
+        for k in (1, 3):
+
+            @pl.when(me + offsets[k] < 0)
+            def _(k=k):
+                pl.semaphore_wait(ready_sems.at[k], 1)
+                sends[k].start()
 
     copies[6].wait()
     copies[8].wait()
@@ -231,6 +256,8 @@
         return carry
 
     def beside(odd, first_block, step, carry):
+        if odd:
+            pl.when(step == 2)(send_late)
         for v in range(16):
             ghost_unit(16 * step + v, odd)
         own_block(first_block + step)
@@ -358,6 +385,7 @@
             pltpu.SemaphoreType.DMA((9,)),
             pltpu.SemaphoreType.DMA((4,)),
             pltpu.SemaphoreType.DMA((4,)),
+            pltpu.SemaphoreType.REGULAR((4,)),
         ],
         compiler_params=pltpu.CompilerParams(
             collective_id=0, has_side_effects=True, vmem_limit_bytes=32 * 1024 * 1024

time: 20.6 us -> 23.1 us (1.12)
  the two profiles are of different devices: /device:TPU:0 before, /device:TPU:30 now
where the time goes in v4:
time: 23.1 us; the launch traced here: 23 us
  Pallas kernels  20.8 us (90%)
  local copies, waits for them, and re-layouts  1.53 us (7%)
  between operations  0.64 us (3%)
    pallas_call x1, Pallas kernels, local(): pl.pallas_call(functools.partial(kernel, members), out_shape=(jax.ShapeDt...  20.8 us
    unnamed x2, local copies, waits for them, and re-layouts  1.53 us

profile of v4, /device:TPU:30, one launch (start us, length us, event | category | flops | bytes accessed | tf_op | source)
XLA Modules:
  0.0 23.0 jit_solution(14220803357872196855)
XLA Ops:
  0.6 20.8 %shard_map.104 = (f32[64,128]{1,0:T(8,128)S(1)}, f32[3,8,9216]{2,1,0:T(8,128)S(1)}) custom-call(f32[64,128]{1,0:T(8,128)} %bitcast.6, f32[3,8192]{1,0:T(4,128)} %gradient.1, f32[64,128]{1,0:T(8,128)} %bitcast.7, f32[2,8192]{1,0:T(2,128)} %history.1, s32[64,128]{1,0:T(8,128)} %bitcast.8, s32[6,8192]{1,0:T(8,128)} %neighbors.1, f32[6,8192]{1,0:T(8,128)} %weights.1, ...), custom_call_target="tpu_custom_call" | custom-call | tf_op jit(solution)/shard_map/pallas_call | solution.py:352
  21.5 0.6 %copy.13 = f32[8192]{0:T(1024)} copy(f32[8192]{0:T(1024)S(1)} %bitcast.5) | data formatting | bytes 65536
  22.1 0.9 %copy.14 = f32[3,8,9216]{2,1,0:T(8,128)} copy(f32[3,8,9216]{2,1,0:T(8,128)S(1)} %get-tuple-element.9) | data formatting | bytes 1769472

commit v5 on v3

--- a/solution.py
+++ b/solution.py
@@ -18,8 +18,9 @@
 FIELDS = 8
 OWN_AT = 8
 WINDOW = 96
-PACKET = 24 + FIELDS * MARGIN_ROWS
 FLOAT = jnp.float32
+HOT = 24
+PART = 80
 
 
 def lookup(row, lanes):
@@ -64,9 +65,12 @@
     shifted,
     outgoing,
     incoming,
+    edges,
+    beyond,
     local_sems,
     send_sems,
     recv_sems,
+    ready_sems,
 ):
     me = lax.axis_index("dom")
     far = members // 8
@@ -87,14 +91,22 @@
         pltpu.make_async_copy(source, target, local_sems.at[i])
         for i, (source, target) in enumerate(pairs)
     ]
-    for copy in copies:
+    for copy in copies[:2]:
         copy.start()
 
+    mesh_id = pl.DeviceIdType.MESH
     barrier = pltpu.get_barrier_semaphore()
-    for target in targets:
-        pl.semaphore_signal(
-            barrier, inc=1, device_id=(target,), device_id_type=pl.DeviceIdType.MESH
-        )
+
+    def signal(semaphore, k):
+        pl.semaphore_signal(semaphore, inc=1, device_id=(targets[k],), device_id_type=mesh_id)
+
+    last_line = members - far
+    pl.when(me < members - 1)(lambda: signal(barrier, 0))
+    signal(barrier, 1)
+    pl.when(me < last_line)(lambda: signal(barrier, 2))
+    pl.when(me < far)(lambda: signal(barrier, 3))
+    for copy in copies[2:]:
+        copy.start()
 
     copies[0].wait()
     copies[1].wait()
@@ -129,26 +141,64 @@
             window[5 + c, at, :] = history_t[pl.ds(16 * b + c, 8, stride=2), :]
         window[7, at, :] = flags_v[own, :].astype(FLOAT)
     for f in range(FIELDS):
-        at = 24 + MARGIN_ROWS * f
+        at = MARGIN_ROWS * f
         last = OWN_AT + ROWS - MARGIN_ROWS
-        outgoing[0, at : at + MARGIN_ROWS, :] = window[f, last : last + MARGIN_ROWS, :]
-        outgoing[1, at : at + MARGIN_ROWS, :] = window[f, OWN_AT : OWN_AT + MARGIN_ROWS, :]
-
-    pl.semaphore_wait(barrier, 4)
-    sends = []
-    for k in range(4):
-        size = PACKET if k < 2 else 24
-        sends.append(
-            pltpu.make_async_remote_copy(
-                src_ref=outgoing.at[k, pl.ds(0, size)],
-                dst_ref=incoming.at[k, pl.ds(0, size)],
-                send_sem=send_sems.at[k],
-                recv_sem=recv_sems.at[k],
-                device_id=(targets[k],),
-                device_id_type=pl.DeviceIdType.MESH,
-            )
+        edges[0, at : at + MARGIN_ROWS, :] = window[f, last : last + MARGIN_ROWS, :]
+        edges[1, at : at + MARGIN_ROWS, :] = window[f, OWN_AT : OWN_AT + MARGIN_ROWS, :]
+
+    def packet(k, target):
+        return pltpu.make_async_remote_copy(
+            src_ref=outgoing.at[k],
+            dst_ref=incoming.at[k],
+            send_sem=send_sems.at[k],
+            recv_sem=recv_sems.at[k],
+            device_id=(target,),
+            device_id_type=mesh_id,
         )
-        sends[k].start()
+
+    margins = [
+        pltpu.make_async_remote_copy(
+            src_ref=edges.at[k],
+            dst_ref=beyond.at[k],
+            send_sem=send_sems.at[4 + k],
+            recv_sem=recv_sems.at[4 + k],
+            device_id=(targets[k],),
+            device_id_type=mesh_id,
+        )
+        for k in range(2)
+    ]
+    sends = [packet(k, targets[k]) for k in range(4)]
+
+    heard = 3 - (me < far).astype(jnp.int32) - (me == 0).astype(jnp.int32)
+    pl.semaphore_wait(barrier, heard + (me >= last_line).astype(jnp.int32))
+    pl.when(me >= far)(lambda: signal(ready_sems.at[2], 3))
+    pl.when(me >= last_line)(lambda: signal(ready_sems.at[3], 2))
+    pl.when(me == members - 1)(lambda: signal(ready_sems.at[1], 0))
+    sends[0].start()
+    pl.when(me > 0)(sends[1].start)
+    pl.when(me >= far)(sends[3].start)
+    pl.when(me >= last_line)(sends[2].start)
+    margins[0].start()
+    pl.when(me > 0)(margins[1].start)
+
+    def send_late(k, where):
+        @pl.when(where)
+        def _():
+            pl.semaphore_wait(ready_sems.at[k], 1)
+            sends[k].start()
+            if k == 1:
+                margins[1].start()
+
+    start, end = me == 0, me == members - 1
+    order = [
+        jnp.where(start, 1, 0),
+        jnp.where(start, 3, jnp.where(end, 2, 1)),
+        jnp.where(start, 2, jnp.where((me < far) | end, 3, 2)),
+        jnp.where(start, 0, jnp.where(end, 1, jnp.where(me < far, 2, 3))),
+    ]
+
+    def arrived(k):
+        packet(k, targets[0]).wait_recv()
 
     copies[6].wait()
     copies[8].wait()
@@ -156,20 +206,24 @@
         index = neighbors_v[:, 128 * t : 128 * t + 128]
         neighbors_t[8 * t : 8 * t + 6, :] = index
         half = (index >> 12) & 1
-        column_t[8 * t : 8 * t + 6, :] = ((index & 127) + 128 * half + 256 * (index >> 13)).astype(FLOAT)
-        row_t[8 * t : 8 * t + 6, :] = (index >> 7) & 31
+        row = (index >> 7) & 31
+        elsewhere = jnp.where(jnp.logical_or(index >= ELEMENTS, row >= HOT), 256, 0)
+        column_t[8 * t : 8 * t + 6, :] = ((index & 127) + 128 * half + elsewhere).astype(FLOAT)
+        row_t[8 * t : 8 * t + 6, :] = row
         weights_t[8 * t : 8 * t + 6, :] = weights_v[:, 128 * t : 128 * t + 128]
-    for c in range(3):
-        for half in range(2):
-            for q in range(2):
-                part = jnp.concatenate(
-                    [gradient_t[pl.ds(4 * (32 * half + 16 * q + 8 * u) + c, 8, stride=4), :] for u in range(2)], axis=0
-                )
-                for s in range(3):
-                    piece = part.astype(jnp.bfloat16)
-                    at = 96 * s + 32 * c + 16 * q
-                    table[at : at + 16, 128 * half : 128 * half + 128] = piece
-                    part = part - piece.astype(FLOAT)
+    for half in range(2):
+        groups = [
+            gradient_t[pl.ds(4 * (32 * half + 8 * q) + c, 8, stride=4), :]
+            for c in range(3)
+            for q in range(HOT // 8)
+        ] + [jnp.zeros((8, 128), FLOAT)]
+        for g in range(0, len(groups), 2):
+            part = jnp.concatenate(groups[g : g + 2], axis=0)
+            for s in range(3):
+                piece = part.astype(jnp.bfloat16)
+                at = PART * s + 8 * g
+                table[at : at + 16, 128 * half : 128 * half + 128] = piece
+                part = part - piece.astype(FLOAT)
     steps[...] = lax.broadcasted_iota(jnp.int32, (256, 128), 0).astype(FLOAT).astype(jnp.bfloat16)
     sublane = lax.broadcasted_iota(jnp.int32, (8, 128), 0)
     one, zero = jnp.ones((), jnp.bfloat16), jnp.zeros((), jnp.bfloat16)
@@ -177,10 +231,10 @@
     def wide(ref, at):
         return jnp.broadcast_to(ref[pl.ds(at, 1), :], (8, 128))
 
-    def own_block(block):
-        for p in range(4):
+    def own_pairs(first, number):
+        for p in range(number):
             sums = [jnp.zeros((8, 128), FLOAT) for _ in range(2)]
-            rows = [8 * block + 2 * p + e for e in range(2)]
+            rows = [2 * (first + p) + e for e in range(2)]
             for m in range(6):
                 hot = []
                 for e in range(2):
@@ -189,15 +243,15 @@
                     hot.append(jnp.where(column == steps[...], one, zero))
                 hot = jnp.concatenate(hot, axis=1)
                 got = jnp.dot(table[...], hot, preferred_element_type=FLOAT)
-                got = got[0:96] + got[96:192] + got[192:288]
+                got = got[0 : 3 * HOT] + got[PART : PART + 3 * HOT] + got[2 * PART : 2 * PART + 3 * HOT]
                 for e in range(2):
                     row = wide(row_t, 8 * rows[e] + m)
-                    hits = [row == sublane + 8 * g for g in range(4)]
+                    hits = [row == sublane + 8 * g for g in range(HOT // 8)]
                     square = None
                     for c in range(3):
                         value = jnp.zeros((8, 128), FLOAT)
-                        for g in range(4):
-                            at = 32 * c + 8 * g
+                        for g in range(HOT // 8):
+                            at = HOT * c + 8 * g
                             value = jnp.where(hits[g], got[at : at + 8, 128 * e : 128 * e + 128], value)
                         jump = wide(gradient_t, 4 * rows[e] + c) - value
                         square = jump * jump if square is None else square + jump * jump
@@ -206,56 +260,87 @@
             for e in range(2):
                 own_sum[pl.ds(rows[e], 1), :] = jnp.sum(sums[e], axis=0, keepdims=True)
 
-    def ghost_unit(unit, odd):
+    def unit_terms(unit, group, found_rows, inside):
         block = unit // 6
         m = unit - 6 * block
         base = pl.multiple_of(block * 64, 64)
         index = neighbors_t[pl.ds(base + m, 8, stride=8), :]
         lanes, rows = index & 127, index >> 7
         totals = [jnp.zeros((8, 128), FLOAT) for _ in range(3)]
-        for k in (odd, 2 + odd):
-            for s in range(8):
-                hit = rows == ROWS + 8 * k + s
-                for c in range(3):
-                    got = lookup(incoming[k, 8 * c + s : 8 * c + s + 1, :], lanes)
-                    totals[c] = jnp.where(hit, got, totals[c])
+        for row, entries in found_rows:
+            hit = rows == row
+            for c in range(3):
+                totals[c] = jnp.where(hit, lookup(entries(c), lanes), totals[c])
         square = None
         for c in range(3):
             jump = gradient_t[pl.ds(pl.multiple_of(block * 32, 32) + c, 8, stride=4), :] - totals[c]
             square = jump * jump if square is None else square + jump * jump
-        here = jnp.logical_and(rows >= ROWS, ((rows >> 3) & 1) == odd)
-        terms[odd, unit] = jnp.where(here, weights_t[pl.ds(base + m, 8, stride=8), :] * square, 0.0)
-
-    def alone(block, carry):
-        own_block(block)
+        weight = weights_t[pl.ds(base + m, 8, stride=8), :]
+        terms[group, unit] = jnp.where(inside(rows), weight * square, 0.0)
+
+    def rest_unit(unit):
+        found_rows = [
+            (r, lambda c, r=r: gradient_v[c : c + 1, 128 * r : 128 * r + 128])
+            for h in range(2)
+            for r in range(32 * h + HOT, 32 * h + 32)
+        ]
+        unit_terms(unit, 3, found_rows, lambda rows: jnp.logical_and(rows < ROWS, (rows & 31) >= HOT))
+
+    def ghost_unit(unit, group, sources):
+        found_rows = [
+            (ROWS + 8 * k + s, lambda c, k=k, s=s: incoming[k, 8 * c + s : 8 * c + s + 1, :])
+            for k in sources
+            for s in range(8)
+        ]
+
+        def inside(rows):
+            return functools.reduce(jnp.logical_or, [(rows >> 3) == 8 + k for k in sources])
+
+        unit_terms(unit, group, found_rows, inside)
+
+    def rest(step, carry):
+        for v in range(16):
+            rest_unit(16 * step + v)
+        own_pairs(4 * step, 4)
         return carry
 
-    def beside(odd, first_block, step, carry):
+    def pair(step, carry):
+        send_late(2, (step == 1) & (me < last_line))
         for v in range(16):
-            ghost_unit(16 * step + v, odd)
-        own_block(first_block + step)
+            ghost_unit(16 * step + v, 0, order[:2])
+        own_pairs(12 + 4 * step, 4)
         return carry
 
-    lax.fori_loop(0, 2, alone, 0)
-    sends[1].wait_recv()
-    sends[3].wait_recv()
-    lax.fori_loop(0, 3, functools.partial(beside, 1, 2), 0)
-    sends[0].wait_recv()
-    sends[2].wait_recv()
-    lax.fori_loop(0, 3, functools.partial(beside, 0, 5), 0)
+    lax.fori_loop(0, 3, rest, 0)
+    arrived(order[0])
+    arrived(order[1])
+    lax.fori_loop(0, 3, pair, 0)
+    send_late(3, me < far)
+    arrived(order[2])
+    for v in range(48):
+        ghost_unit(v, 1, order[2:3])
+    own_pairs(24, 4)
+    send_late(1, start)
+    arrived(order[3])
+    for v in range(48):
+        ghost_unit(v, 2, order[3:])
+    own_pairs(28, 4)
     for block in range(BLOCKS):
         total = own_sum[8 * block : 8 * block + 8, :]
         for m in range(6):
-            total = total + (terms[0, 6 * block + m] + terms[1, 6 * block + m])
+            for group in range(4):
+                total = total + terms[group, 6 * block + m]
         indicator[8 * block : 8 * block + 8, :] = total
 
+    for margin in margins:
+        margin.wait_recv()
     for f in range(FIELDS):
-        at = 24 + MARGIN_ROWS * f
-        window[f, OWN_AT - MARGIN_ROWS : OWN_AT, :] = incoming[0, at : at + MARGIN_ROWS, :]
+        at = MARGIN_ROWS * f
+        window[f, OWN_AT - MARGIN_ROWS : OWN_AT, :] = beyond[0, at : at + MARGIN_ROWS, :]
         right = OWN_AT + ROWS
         window[f, right : right + 8, :] = jnp.zeros((8, 128), FLOAT)
         window[f, right + 8 : right + 16, :] = jnp.zeros((8, 128), FLOAT)
-        window[f, right : right + MARGIN_ROWS, :] = incoming[1, at : at + MARGIN_ROWS, :]
+        window[f, right : right + MARGIN_ROWS, :] = beyond[1, at : at + MARGIN_ROWS, :]
     copies[7].wait()
     owners = lax.broadcasted_iota(jnp.int32, (1, 128), 1)
     held = counts_v[...]
@@ -292,7 +377,7 @@
         children[0, :, at] = jnp.where(kept, moved, 0.0)
         children[1, :, at] = jnp.where(kept, row[5], 0.0)
         children[2, :, at] = jnp.where(kept, row[6], 0.0)
-    for send in sends:
+    for send in sends + margins:
         send.wait_send()
 
 
@@ -347,17 +432,20 @@
             vmem((32, 128), jnp.int32),
             vmem((8 * ROWS, 128), FLOAT),
             vmem((8 * ROWS, 128), jnp.int32),
-            vmem((288, 256), jnp.bfloat16),
+            vmem((3 * PART, 256), jnp.bfloat16),
             vmem((256, 128), jnp.bfloat16),
             vmem(flat, FLOAT),
-            vmem((2, 6 * BLOCKS, 8, 128), FLOAT),
+            vmem((4, 6 * BLOCKS, 8, 128), FLOAT),
             vmem((FIELDS, WINDOW, 128), FLOAT),
             vmem((FIELDS, OUT_ROWS, 128), FLOAT),
-            vmem((4, PACKET, 128), FLOAT),
-            vmem((4, PACKET, 128), FLOAT),
+            vmem((4, 24, 128), FLOAT),
+            vmem((4, 24, 128), FLOAT),
+            vmem((2, FIELDS * MARGIN_ROWS, 128), FLOAT),
+            vmem((2, FIELDS * MARGIN_ROWS, 128), FLOAT),
             pltpu.SemaphoreType.DMA((9,)),
-            pltpu.SemaphoreType.DMA((4,)),
-            pltpu.SemaphoreType.DMA((4,)),
+            pltpu.SemaphoreType.DMA((6,)),
+            pltpu.SemaphoreType.DMA((6,)),
+            pltpu.SemaphoreType.REGULAR((4,)),
         ],
         compiler_params=pltpu.CompilerParams(
             collective_id=0, has_side_effects=True, vmem_limit_bytes=32 * 1024 * 1024

time: 20.6 us -> 19.2 us (0.932)
  the two profiles are of different devices: /device:TPU:0 before, /device:TPU:6 now
where the time goes in v5:
time: 19.2 us; the launch traced here: 19.1 us
  Pallas kernels  16.9 us (88%)
  local copies, waits for them, and re-layouts  1.53 us (8%)
  between operations  0.64 us (3%)
    pallas_call x1, Pallas kernels, local(): pl.pallas_call(functools.partial(kernel, members), out_shape=(jax.ShapeDt...  16.9 us
    unnamed x2, local copies, waits for them, and re-layouts  1.53 us

profile of v5, /device:TPU:6, one launch (start us, length us, event | category | flops | bytes accessed | tf_op | source)
XLA Modules:
  0.0 19.1 jit_solution(6950606753990593513)
XLA Ops:
  0.6 16.9 %shard_map.104 = (f32[64,128]{1,0:T(8,128)S(1)}, f32[3,8,9216]{2,1,0:T(8,128)S(1)}) custom-call(f32[64,128]{1,0:T(8,128)} %bitcast.6, f32[3,8192]{1,0:T(4,128)} %gradient.1, f32[64,128]{1,0:T(8,128)} %bitcast.7, f32[2,8192]{1,0:T(2,128)} %history.1, s32[64,128]{1,0:T(8,128)} %bitcast.8, s32[6,8192]{1,0:T(8,128)} %neighbors.1, f32[6,8192]{1,0:T(8,128)} %weights.1, ...), custom_call_target="tpu_custom_call" | custom-call | tf_op jit(solution)/shard_map/pallas_call | solution.py:410
  17.5 0.6 %copy.13 = f32[8192]{0:T(1024)} copy(f32[8192]{0:T(1024)S(1)} %bitcast.5) | data formatting | bytes 65536
  18.1 0.9 %copy.14 = f32[3,8,9216]{2,1,0:T(8,128)} copy(f32[3,8,9216]{2,1,0:T(8,128)S(1)} %get-tuple-element.9) | data formatting | bytes 1769472

commit v6 on v5

--- a/solution.py
+++ b/solution.py
@@ -15,6 +15,7 @@
 MARGIN_ROWS = MARGIN // 128
 CAPACITY = ELEMENTS + 2 * MARGIN
 OUT_ROWS = CAPACITY // 128
+CHUNK = 24
 FIELDS = 8
 OWN_AT = 8
 WINDOW = 96
@@ -39,8 +40,10 @@
     weights,
     ghost_send,
     counts,
-    indicator,
-    children,
+    window,
+    own_sum,
+    terms,
+    counts_out,
     density_v,
     gradient_v,
     size_v,
@@ -59,10 +62,6 @@
     row_t,
     table,
     steps,
-    own_sum,
-    terms,
-    window,
-    shifted,
     outgoing,
     incoming,
     edges,
@@ -325,13 +324,6 @@
     for v in range(48):
         ghost_unit(v, 2, order[3:])
     own_pairs(28, 4)
-    for block in range(BLOCKS):
-        total = own_sum[8 * block : 8 * block + 8, :]
-        for m in range(6):
-            for group in range(4):
-                total = total + terms[group, 6 * block + m]
-        indicator[8 * block : 8 * block + 8, :] = total
-
     for margin in margins:
         margin.wait_recv()
     for f in range(FIELDS):
@@ -342,8 +334,15 @@
         window[f, right + 8 : right + 16, :] = jnp.zeros((8, 128), FLOAT)
         window[f, right : right + MARGIN_ROWS, :] = beyond[1, at : at + MARGIN_ROWS, :]
     copies[7].wait()
+    counts_out[...] = counts_v[...]
+    for send in sends + margins:
+        send.wait_send()
+
+
+def finish(members, window, own_sum, terms, counts, indicator, children, shifted, indicator_v, children_v, sems):
+    me = lax.axis_index("dom")
     owners = lax.broadcasted_iota(jnp.int32, (1, 128), 1)
-    held = counts_v[...]
+    held = counts[...]
     begin = jnp.sum(jnp.where(owners < me, held, 0))
     count = jnp.sum(jnp.where(owners == me, held, 0))
     count = jnp.minimum(count, members * ELEMENTS - begin)
@@ -367,6 +366,7 @@
     child = lax.broadcasted_iota(jnp.int32, (8, 128), 0)
     signs = [(2 * ((child >> c) & 1) - 1).astype(FLOAT) for c in range(3)]
     eldest = child == 0
+    copies = []
     for t in range(OUT_ROWS):
         row = [jnp.broadcast_to(shifted[f, t : t + 1, :], (8, 128)) for f in range(FIELDS)]
         slope = signs[0] * row[1] + signs[1] * row[2] + signs[2] * row[3]
@@ -374,11 +374,24 @@
         kept = jnp.logical_or(refined, eldest)
         at = slice(128 * t, 128 * t + 128)
         moved = jnp.where(refined, row[0] + row[4] * slope, row[0])
-        children[0, :, at] = jnp.where(kept, moved, 0.0)
-        children[1, :, at] = jnp.where(kept, row[5], 0.0)
-        children[2, :, at] = jnp.where(kept, row[6], 0.0)
-    for send in sends + margins:
-        send.wait_send()
+        children_v[0, :, at] = jnp.where(kept, moved, 0.0)
+        children_v[1, :, at] = jnp.where(kept, row[5], 0.0)
+        children_v[2, :, at] = jnp.where(kept, row[6], 0.0)
+        if (t + 1) % CHUNK == 0:
+            part = pl.ds(128 * (t + 1 - CHUNK), 128 * CHUNK)
+            out = pltpu.make_async_copy(children_v.at[:, :, part], children.at[:, :, part], sems.at[t // CHUNK])
+            out.start()
+            copies.append(out)
+    for block in range(BLOCKS):
+        total = own_sum[8 * block : 8 * block + 8, :]
+        for m in range(6):
+            for group in range(4):
+                total = total + terms[group, 6 * block + m]
+        indicator_v[8 * block : 8 * block + 8, :] = total
+    out = pltpu.make_async_copy(indicator_v, indicator, sems.at[OUT_ROWS // CHUNK])
+    out.start()
+    for copy in copies + [out]:
+        copy.wait()
 
 
 def local(
@@ -407,14 +420,16 @@
         new_counts.reshape(1, 128),
     )
     operands = [pltpu.with_memory_space_constraint(x, pltpu.HBM) for x in operands]
-    indicator, children = pl.pallas_call(
+    handed = pl.pallas_call(
         functools.partial(kernel, members),
         out_shape=(
-            jax.ShapeDtypeStruct(flat, FLOAT),
-            jax.ShapeDtypeStruct((3, 8, CAPACITY), FLOAT),
+            vmem((FIELDS, WINDOW, 128), FLOAT),
+            vmem(flat, FLOAT),
+            vmem((4, 6 * BLOCKS, 8, 128), FLOAT),
+            vmem((1, 128), jnp.int32),
         ),
         in_specs=[pl.BlockSpec(memory_space=pltpu.HBM)] * 9,
-        out_specs=(pl.BlockSpec(memory_space=vmem),) * 2,
+        out_specs=(pl.BlockSpec(memory_space=vmem),) * 4,
         scratch_shapes=[
             vmem(flat, FLOAT),
             vmem((3, ELEMENTS), FLOAT),
@@ -434,10 +449,6 @@
             vmem((8 * ROWS, 128), jnp.int32),
             vmem((3 * PART, 256), jnp.bfloat16),
             vmem((256, 128), jnp.bfloat16),
-            vmem(flat, FLOAT),
-            vmem((4, 6 * BLOCKS, 8, 128), FLOAT),
-            vmem((FIELDS, WINDOW, 128), FLOAT),
-            vmem((FIELDS, OUT_ROWS, 128), FLOAT),
             vmem((4, 24, 128), FLOAT),
             vmem((4, 24, 128), FLOAT),
             vmem((2, FIELDS * MARGIN_ROWS, 128), FLOAT),
@@ -451,6 +462,20 @@
             collective_id=0, has_side_effects=True, vmem_limit_bytes=32 * 1024 * 1024
         ),
     )(*operands)
+    handed = [pltpu.with_memory_space_constraint(x, vmem) for x in handed]
+    indicator, children = pl.pallas_call(
+        functools.partial(finish, members),
+        out_shape=(pltpu.HBM(flat, FLOAT), pltpu.HBM((3, 8, CAPACITY), FLOAT)),
+        in_specs=[pl.BlockSpec(memory_space=vmem)] * 4,
+        out_specs=(pl.BlockSpec(memory_space=pltpu.HBM),) * 2,
+        scratch_shapes=[
+            vmem((FIELDS, OUT_ROWS, 128), FLOAT),
+            vmem(flat, FLOAT),
+            vmem((3, 8, CAPACITY), FLOAT),
+            pltpu.SemaphoreType.DMA((OUT_ROWS // CHUNK + 1,)),
+        ],
+        compiler_params=pltpu.CompilerParams(vmem_limit_bytes=8 * 1024 * 1024),
+    )(*handed)
     return indicator.reshape(ELEMENTS), children
 
 

time: 19.2 us -> 18.5 us (0.964)
  local copies, waits for them, and re-layouts: 1.53 us -> 0 us
  Pallas kernels: 16.9 us -> 17.7 us
    unnamed x2 -> x0, local copies, waits for them, and re-layouts: 1.53 us -> none
    pallas_call x1 -> x2, Pallas kernels: 16.9 us -> 17.7 us  [the longest x1 16.4 us: local(): pl.pallas_call(functools.partial(kernel, members), out_shape=(vmem((FIELD...]
where the time goes in v6:
time: 18.5 us; the launch traced here: 18.4 us
  Pallas kernels  17.7 us (96%)
  between operations  0.64 us (3%)
    pallas_call x1, Pallas kernels, local(): pl.pallas_call(functools.partial(kernel, members), out_shape=(vmem((FIELD...  16.4 us
    pallas_call x1, Pallas kernels, local(): pl.pallas_call(functools.partial(finish, members), out_shape=(pltpu.HBM(f...  1.38 us

profile of v6, /device:TPU:6, one launch (start us, length us, event | category | flops | bytes accessed | tf_op | source)
XLA Modules:
  0.0 18.4 jit_solution(2793088589347605230)
XLA Ops:
  0.6 16.4 %shard_map.104 = (f32[8,96,128]{2,1,0:T(8,128)S(1)}, f32[64,128]{1,0:T(8,128)S(1)}, f32[4,48,8,128]{3,2,1,0:T(8,128)S(1)}, s32[1,128]{1,0:T(1,128)S(1)}) custom-call(f32[64,128]{1,0:T(8,128)} %bitcast.5, f32[3,8192]{1,0:T(4,128)} %gradient.1, f32[64,128]{1,0:T(8,128)} %bitcast.6, f32[2,8192]{1,0:T(2,128)} %history.1, s32[64,128]{1,0:T(8,128)} %bitcast.7, ...), custom_call_target="tpu_custom_call" | custom-call | tf_op jit(solution)/shard_map/pallas_call | solution.py:423
  17.0 1.4 %shard_map.105 = (f32[64,128]{1,0:T(8,128)}, f32[3,8,9216]{2,1,0:T(8,128)}) custom-call(f32[8,96,128]{2,1,0:T(8,128)S(1)} %get-tuple-element.8.window, f32[64,128]{1,0:T(8,128)S(1)} %get-tuple-element.9.own_sum, f32[4,48,8,128]{3,2,1,0:T(8,128)S(1)} %get-tuple-element.10.terms, s32[1,128]{1,0:T(1,128)S(1)} %get-tuple-element.11.counts), custom_call_target="tpu_custom_call" | custom-call | tf_op jit(solution)/shard_map/pallas_call | solution.py:466

commit v7 on v6

--- a/solution.py
+++ b/solution.py
@@ -353,8 +353,9 @@
     slot = lax.broadcasted_iota(jnp.int32, (8, 128), 0) * 128 + lane
     turned = (lane + turn) & 127
     low = lane < 128 - turn
-    for f in range(FIELDS):
-        for b in range(OUT_ROWS // 8):
+
+    def shift(b):
+        for f in range(FIELDS):
             here = window[f, pl.ds(first + 8 * b, 8), :]
             there = window[f, pl.ds(first + 8 * b + 1, 8), :]
             both = [jnp.take_along_axis(v, turned, axis=1, mode="promise_in_bounds") for v in (here, there)]
@@ -368,6 +369,9 @@
     eldest = child == 0
     copies = []
     for t in range(OUT_ROWS):
+        if t % CHUNK == 0:
+            for b in range(t // 8, (t + CHUNK) // 8):
+                shift(b)
         row = [jnp.broadcast_to(shifted[f, t : t + 1, :], (8, 128)) for f in range(FIELDS)]
         slope = signs[0] * row[1] + signs[1] * row[2] + signs[2] * row[3]
         refined = row[7] > 0.0

time: 18.5 us -> 18.4 us (level)
  no operation moved by 1% of the time
where the time goes in v7:
time: 18.4 us; the launch traced here: 18.3 us
  Pallas kernels  17.6 us (96%)
  between operations  0.64 us (3%)
    pallas_call x1, Pallas kernels, local(): pl.pallas_call(functools.partial(kernel, members), out_shape=(vmem((FIELD...  16.4 us
    pallas_call x1, Pallas kernels, local(): pl.pallas_call(functools.partial(finish, members), out_shape=(pltpu.HBM(f...  1.26 us

profile of v7, /device:TPU:6, one launch (start us, length us, event | category | flops | bytes accessed | tf_op | source)
XLA Modules:
  0.0 18.3 jit_solution(2355257919456959982)
XLA Ops:
  0.6 16.4 %shard_map.104 = (f32[8,96,128]{2,1,0:T(8,128)S(1)}, f32[64,128]{1,0:T(8,128)S(1)}, f32[4,48,8,128]{3,2,1,0:T(8,128)S(1)}, s32[1,128]{1,0:T(1,128)S(1)}) custom-call(f32[64,128]{1,0:T(8,128)} %bitcast.5, f32[3,8192]{1,0:T(4,128)} %gradient.1, f32[64,128]{1,0:T(8,128)} %bitcast.6, f32[2,8192]{1,0:T(2,128)} %history.1, s32[64,128]{1,0:T(8,128)} %bitcast.7, ...), custom_call_target="tpu_custom_call" | custom-call | tf_op jit(solution)/shard_map/pallas_call | solution.py:427
  17.0 1.3 %shard_map.105 = (f32[64,128]{1,0:T(8,128)}, f32[3,8,9216]{2,1,0:T(8,128)}) custom-call(f32[8,96,128]{2,1,0:T(8,128)S(1)} %get-tuple-element.8.window, f32[64,128]{1,0:T(8,128)S(1)} %get-tuple-element.9.own_sum, f32[4,48,8,128]{3,2,1,0:T(8,128)S(1)} %get-tuple-element.10.terms, s32[1,128]{1,0:T(1,128)S(1)} %get-tuple-element.11.counts), custom_call_target="tpu_custom_call" | custom-call | tf_op jit(solution)/shard_map/pallas_call | solution.py:470
